TPU v7x, 32 devices: a whole 2x2x4 slice. The times are simulated.
32 devices in a mesh: fsdp: 4 (over y, core), dp: 4 (over z), engine: 2 (over x).
Axes of the slice: x: 2, y: 2, z: 4, core: 2. Of those that a mesh axis runs over, the one named last changes fastest.
Arguments:
- activations: bfloat16 [4096, 8192], P(('fsdp', 'dp', 'engine')), may hold values from -6 to 6
- upstream: bfloat16 [4096, 512], P(('fsdp', 'dp', 'engine')), may hold values from -6 to 6
- segment: int32 [32, 128], P(('fsdp', 'dp', 'engine')), may hold values from 0 to 3, never falling along the last dimension, each value on 1 to 64 neighbouring positions
- reward: float32 [128], P(('fsdp', 'dp', 'engine')), may hold values from -6 to 6
- prompt_group_index: int32 [128, 1], P(('fsdp', 'dp', 'engine')), may hold values from 0 to 7
- frozen_value_weight: bfloat16 [8192, 512], P(('fsdp', 'engine')), may hold values from -0.25 to 0.25
- adapter_down_weight: bfloat16 [8192, 64], P('fsdp'), may hold values from -0.0625 to 0.0625
- adapter_up_weight: bfloat16 [64, 512], replicated, may hold values from -0.75 to 0.75
Outputs:
- input_gradient: bfloat16 [4096, 8192], P(('fsdp', 'dp', 'engine'))
- step_down: float32 [8192, 64], P('fsdp')
- step_up: float32 [64, 512], replicated
Inputs may be any that keep to these rules, and one draw needn't show every extreme that they name: `segment`: within each row the numbers never fall and every rollout 0 to 3 has at least one token. `prompt_group_index`: every group has at least one rollout.
All inputs are finite; a program needn't handle non-finite values.
Results may differ from a plain program's by a relative error of at most 0.011.
Values may be sent and summed in bfloat16 or wider, within the bound.
A program may use at most 64 MiB of HBM per device.

v0:
```python
import jax
import jax.numpy as jnp
from jax import lax
from jax.sharding import PartitionSpec as P

MODEL_WIDTH = 8192
VALUE_OUTPUTS = 512
ADAPTER_RANK = 64
GSIZE = 16


adapter_scale = 2.0
HIGH = lax.Precision.HIGHEST


def local(
    activations,
    upstream,
    segment,
    reward,
    prompt_group_index,
    frozen_value_weight,
    adapter_down_weight,
    adapter_up_weight,
):
    device_count = lax.axis_size("fsdp") * lax.axis_size("dp") * lax.axis_size("engine")
    group_total = reward.shape[0] * device_count // GSIZE
    labels = jnp.arange(group_total, dtype=jnp.int32)
    member = (prompt_group_index == labels[None, :]).astype(jnp.float32)
    group_sum = jnp.dot(reward, member, precision=HIGH)
    group_count = jnp.sum(member, axis=0)
    group_sum, group_count = lax.psum((group_sum, group_count), ("fsdp", "dp", "engine"))
    advantage = reward - jnp.dot(member, group_sum / group_count, precision=HIGH)
    seq_ids = jnp.arange(reward.shape[0], dtype=jnp.int32)
    token_member = (segment[0][:, None] == seq_ids[None, :]).astype(jnp.float32)
    token_adv = jnp.dot(token_member, advantage, precision=HIGH)
    advantage_weighted = (upstream.astype(jnp.float32) * token_adv[:, None]).astype(jnp.bfloat16)
    contract_trailing = (((1,), (1,)), ((), ()))
    contract_leading = (((0,), (0,)), ((), ()))
    down_complete = lax.all_gather(adapter_down_weight, "fsdp", axis=0, tiled=True)
    lowrank_activation = jnp.dot(
        activations, down_complete, preferred_element_type=jnp.float32
    ).astype(jnp.bfloat16)
    backward_lowrank = lax.dot_general(
        advantage_weighted, adapter_up_weight, contract_trailing, preferred_element_type=jnp.float32
    ).astype(jnp.bfloat16)
    frozen_gradient = lax.dot_general(
        advantage_weighted,
        lax.all_gather(frozen_value_weight, ("fsdp", "engine"), axis=0, tiled=True),
        contract_trailing,
        preferred_element_type=jnp.float32,
    ).astype(jnp.bfloat16)
    adapter_portion = lax.dot_general(
        backward_lowrank, down_complete, contract_trailing, preferred_element_type=jnp.float32
    )
    input_gradient = (frozen_gradient.astype(jnp.float32) + adapter_scale * adapter_portion).astype(
        jnp.bfloat16
    )
    down_gradient = adapter_scale * lax.dot_general(
        activations, backward_lowrank, contract_leading, preferred_element_type=jnp.float32
    )
    up_gradient = adapter_scale * lax.dot_general(
        lowrank_activation, advantage_weighted, contract_leading, preferred_element_type=jnp.float32
    )
    clip_norm = jnp.sqrt(jnp.float32(MODEL_WIDTH * ADAPTER_RANK + ADAPTER_RANK * VALUE_OUTPUTS))
    count_of_rows = adapter_down_weight.shape[0]
    summed_down, summed_up = lax.psum((down_gradient, up_gradient), ("fsdp", "dp", "engine"))
    grad_norm = jnp.sqrt(jnp.sum(summed_down * summed_down) + jnp.sum(summed_up * summed_up))
    factor = jnp.minimum(jnp.float32(1.0), clip_norm / (grad_norm + 1e-06))
    own_rows = lax.dynamic_slice_in_dim(
        summed_down, lax.axis_index("fsdp") * count_of_rows, count_of_rows, 0
    )
    return (input_gradient, factor * own_rows, factor * summed_up)


def solution(mesh):
    return jax.shard_map(
        local,
        mesh=mesh,
        in_specs=(
            P(("fsdp", "dp", "engine"), None),
            P(("fsdp", "dp", "engine"), None),
            P(("fsdp", "dp", "engine"), None),
            P(("fsdp", "dp", "engine")),
            P(("fsdp", "dp", "engine"), None),
            P(("fsdp", "engine"), None),
            P("fsdp", None),
            P(),
        ),
        out_specs=(P(("fsdp", "dp", "engine"), None), P("fsdp", None), P()),
        check_vma=False,
    )
```

profile of v0, /device:TPU:0, one launch (start us, length us, event | category | flops | bytes accessed | tf_op | source)
XLA Modules:
  0.0 236.2 jit_solution(10641079486583767807)
XLA Ops:
  8.0 0.0 copy-start
  8.0 0.0 all-gather.5.cloned.1.call-start
  8.1 0.7 all-gather.5.cloned.1.call-update
  8.7 0.0 all-reduce.4.cloned.1.call-start
  8.8 0.9 convolution_bitcast_fusion.1
  9.7 0.7 convert_reduce_fusion
  10.4 42.0 %all-reduce = (f32[8]{0:T(128)S(1)}, f32[8]{0:T(128)S(1)}) all-reduce(f32[8]{0:T(128)S(1)} %convolution_bitcast_fusion.1, f32[8]{0:T(128)S(1)} %convert_reduce_fusion), channel_id=1, replica_groups=mesh['fsdp'=4,'dp'=4,'engine'=2] {'fsdp','dp','engine'}, use_global_device_ids=true, to_apply=%region_0.0 | all-reduce | flops 16 | bytes 128 | tf_op jit(solution)/shard_map/psum | solution.py:32
  52.4 0.9 fusion.5
  53.2 0.9 convolution_bitcast_fusion.2
  54.1 1.2 convolution_convert_fusion.2
  55.3 0.0 copy-done
  55.3 0.0 copy-start.2
  55.3 1.8 fusion.3
  57.1 0.0 all-gather.5.cloned.1.call-done
  57.1 0.0 copy-done.2
  57.1 2.8 %convolution_multiply_fusion.2 = f32[64,512]{1,0:T(8,128)} fusion(bf16[128,8192]{1,0:T(8,128)(2,1)S(1)} %copy-done, bf16[8192,64]{0,1:T(8,128)(2,1)} %all-gather.5.cloned.1.call-done, bf16[128,512]{1,0:T(8,128)(2,1)S(1)} %copy-done.2, f32[128]{0:T(128)S(1)} %convolution_bitcast_fusion.2), kind=kOutput, calls=%fused_computation.8 | convolution fusion | flops 142843904 | bytes 3408384 | tf_op jit(solution)/shard_map/dot_general | solution.py:62
  59.8 0.0 all-reduce.4.cloned.1.call-update
  59.9 0.0 all-gather.3.cloned.1.call-start
  59.9 0.5 all-gather.3.cloned.1.call-update
  60.4 151.7 %all-reduce.4.cloned.1.call-done = (f32[8192,64]{0,1:T(8,128)}, f32[64,512]{1,0:T(8,128)}) async-done(((f32[8192,64]{0,1:T(8,128)}, f32[64,512]{1,0:T(8,128)}), (f32[8192,64]{0,1:T(8,128)}, f32[64,512]{1,0:T(8,128)})) %all-reduce.4.cloned.1.call-update) | async-done | bytes 2228240 | tf_op jit(solution)/shard_map/psum | solution.py:67
  212.1 0.0 copy-start.3
  212.1 1.6 multiply_reduce_fusion.1
  213.7 2.7 %multiply_reduce_fusion = f32[]{:T(128)} fusion(f32[8192,64]{0,1:T(8,128)} %get-tuple-element.5), kind=kLoop, calls=%fused_computation.7 | loop fusion | flops 1048575 | bytes 2097156 | tf_op jit(solution)/shard_map/reduce_sum | solution.py:68
  217.8 0.0 copy-done.3
  217.9 0.7 broadcast_multiply_fusion
  218.5 1.9 dynamic-slice_multiply_fusion
  220.4 0.0 copy-start.1
  220.4 0.0 all-gather.3.cloned.1.call-done
  220.4 6.3 %fusion.1 = f32[128,8192]{1,0:T(8,128)S(1)} fusion(bf16[8192,512]{1,0:T(8,128)(2,1)} %all-gather.3.cloned.1.call-done, bf16[128,512]{1,0:T(8,128)(2,1)S(1)} %copy-done.2, f32[128]{0:T(128)S(1)} %convolution_bitcast_fusion.2), kind=kOutput, calls=%fused_computation.3 | convolution fusion | flops 1076035584 | bytes 12714496 | tf_op jit(solution)/shard_map/dot_general | solution.py:47
  226.7 0.0 copy-done.1
  226.7 2.1 fusion.2
Async XLA Ops:
  8.0 47.3 %copy-start = (bf16[128,8192]{1,0:T(8,128)(2,1)S(1)}, bf16[128,8192]{1,0:T(8,128)(2,1)}, u32[]{:S(2)}) copy-start(bf16[128,8192]{1,0:T(8,128)(2,1)} %param.8) | copy-start | bytes 6291460
  8.0 49.0 %all-gather.5.cloned.1.call-start = ((), (), s32[]{:S(2)}) async-start(), calls=%async_computation.1 | async-start | bytes 1310720 | tf_op jit(solution)/shard_map/all_gather | solution.py:40
  8.7 203.4 %all-reduce.4.cloned.1.call-start = ((), (), s32[]{:S(2)}) async-start(), calls=%async_computation.2 | async-start | bytes 4456448 | tf_op jit(solution)/shard_map/psum | solution.py:67
  55.3 1.8 copy-start.2
  59.9 160.5 %all-gather.3.cloned.1.call-start = ((), (), s32[]{:S(2)}) async-start(), calls=%async_computation | async-start | bytes 9437184 | tf_op jit(solution)/shard_map/all_gather | solution.py:49
  212.1 5.7 %copy-start.3 = (f32[64,512]{1,0:T(8,128)S(1)}, f32[64,512]{1,0:T(8,128)}, u32[]{:S(2)}) copy-start(f32[64,512]{1,0:T(8,128)} %get-tuple-element.6) | copy-start | bytes 393220
  220.4 6.3 %copy-start.1 = (bf16[8192,64]{0,1:T(8,128)(2,1)S(1)}, bf16[8192,64]{0,1:T(8,128)(2,1)}, u32[]{:S(2)}) copy-start(bf16[8192,64]{0,1:T(8,128)(2,1)} %all-gather.5.cloned.1.call-done) | copy-start | bytes 3145732
Sparse Core Ops, SparseCore 0:
  10.4 19.5 all-gather.4
  60.0 152.0 all-reduce.3
Sparse Core Ops, SparseCore 1:
  62.2 55.1 all-gather.2
where the time goes:
time: 237 us; the launch traced here: 236 us
  waiting for transfers between devices  153 us (65%)
  blocking collectives  42 us (18%)
  between operations  16.9 us (7%)
  matrix products  16.7 us (7%)
  other arithmetic  7.64 us (3%)
    psum x1, waiting for transfers between devices, local(): lax.psum((down_gradient, up_gradient), ('fsdp', 'dp', 'engine'))  152 us
    psum x1, blocking collectives, local(): lax.psum((group_sum, group_count), ('fsdp', 'dp', 'engine'))  42 us
    dot_general x1, matrix products, local(): lax.dot_general(advantage_weighted, lax.all_gather(frozen_value_weight, (...  6.3 us
  transfers between devices with their start and end apart: 3, of which 1 were waited for; matrix products, arithmetic and copies ran while one was open for 6% of the time, Pallas kernels for 0%

commit v1 on v0

v1 whole, which is shorter than its diff:
```python
import functools

import jax
import jax.numpy as jnp
from jax import lax
from jax.experimental import pallas as pl
from jax.experimental.pallas import tpu as pltpu
from jax.sharding import PartitionSpec as P

GSIZE = 16
LANES = 128
SCALE = 2.0
MESH = pl.DeviceIdType.MESH
TRAILING = (((1,), (1,)), ((), ()))
F32 = jnp.float32
BF16 = jnp.bfloat16


def kernel(
    dims,
    act_hbm,
    ups_ref,
    info_ref,
    w_hbm,
    down_ref,
    upw_ref,
    out_hbm,
    sd_ref,
    su_ref,
    act,
    w,
    zinfo,
    pinfo,
    adv,
    uall,
    dall,
    wown,
    gsend,
    grecv,
    usend,
    urecv,
    zs,
    zu,
    fin,
    fu,
    stage,
    load_sem,
    zinfo_s,
    zinfo_r,
    pinfo_s,
    pinfo_r,
    u_s,
    u_r,
    d_s,
    d_r,
    g_s,
    g_r,
    up_s,
    up_r,
    zs_s,
    zs_r,
    zu_s,
    zu_r,
    fin_s,
    fin_r,
    fu_s,
    fu_r,
    out_s,
    out_r,
):
    nf, nd, ne, seqs, groups = dims
    np_ = nf * ne
    f, d, e = lax.axis_index("fsdp"), lax.axis_index("dp"), lax.axis_index("engine")
    p = f * ne + e
    cols = w.shape[0]
    rank, values = upw_ref.shape
    chunks = rank // 8

    def each(count, fn):
        if count <= 8:
            for s in range(1, count):
                fn(s)
        else:

            @pl.loop(1, count)
            def _(s):
                fn(s)

    def plane(s):
        q = lax.rem(p + s, np_)
        return q, {"fsdp": q // ne, "engine": lax.rem(q, ne)}

    def line(s):
        q = lax.rem(d + s, nd)
        return q, {"dp": q}

    def fs(s):
        q = lax.rem(f + s, nf)
        return q, {"fsdp": q}

    def eng(s):
        q = lax.rem(e + s, ne)
        return q, {"engine": q}

    def copy(src, dst, ss, rs, dev):
        return pltpu.make_async_remote_copy(
            src_ref=src, dst_ref=dst, send_sem=ss, recv_sem=rs, device_id=dev, device_id_type=MESH
        )

    def span(q, width):
        return pl.ds(pl.multiple_of(q * width, LANES), width)

    load_act = pltpu.make_async_copy(act_hbm, act, load_sem.at[0])
    load_w = pltpu.make_async_copy(w_hbm, w, load_sem.at[1])
    load_act.start()
    load_w.start()

    barrier = pltpu.get_barrier_semaphore()
    each(nd, lambda s: pl.semaphore_signal(barrier, inc=1, device_id=line(s)[1], device_id_type=MESH))
    each(np_, lambda s: pl.semaphore_signal(barrier, inc=1, device_id=plane(s)[1], device_id_type=MESH))
    pl.semaphore_wait(barrier, nd - 1 + np_ - 1)

    def send(peers, count, src, dst, ss, rs, me):
        def go(s):
            q, dev = peers(s)
            copy(src(q), dst(me), ss.at[q], rs.at[me], dev).start()

        each(count, go)

    def arrive(peers, count, src, dst, ss, rs):
        def go(s):
            q, dev = peers(s)
            copy(src(q), dst(q), ss.at[q], rs.at[q], dev).wait_recv()

        each(count, go)

    def sent(peers, count, src, dst, ss, rs, me):
        def go(s):
            q, dev = peers(s)
            copy(src(q), dst(me), ss.at[q], rs.at[me], dev).wait_send()

        each(count, go)

    zi = (line, nd, lambda q: info_ref, lambda q: zinfo.at[q], zinfo_s, zinfo_r)
    pi = (plane, np_, lambda q: zinfo, lambda q: pinfo.at[q], pinfo_s, pinfo_r)
    ua = (plane, np_, lambda q: ups_ref, lambda q: uall.at[q], u_s, u_r)
    da = (fs, nf, lambda q: down_ref, lambda q: dall.at[q], d_s, d_r)
    gr = (plane, np_, lambda q: gsend.at[q], lambda q: grecv.at[q], g_s, g_r)
    ur = (plane, np_, lambda q: usend.at[q], lambda q: urecv.at[q], up_s, up_r)
    zg = (line, nd, lambda q: zs.at[d], lambda q: zs.at[q], zs_s, zs_r)
    zp = (line, nd, lambda q: zu.at[d], lambda q: zu.at[q], zu_s, zu_r)
    fg = (eng, ne, lambda q: fin.at[e], lambda q: fin.at[q], fin_s, fin_r)
    fp = (plane, np_, lambda q: fu.at[p], lambda q: fu.at[q], fu_s, fu_r)
    og = (plane, np_, lambda q: stage.at[q], lambda q: out_hbm.at[:, span(q, cols)], out_s, out_r)

    send(*zi, d)
    zinfo[d] = info_ref[...]
    arrive(*zi)
    send(*pi, p)
    send(*ua, p)
    send(*da, f)
    pinfo[p] = zinfo[...]
    uall[p] = ups_ref[...]
    dall[f] = down_ref[...]
    arrive(*pi)

    rewards = pinfo[:, :, 0, :]
    labels = pinfo[:, :, 1, :]

    def group_mean(g, mean):
        hit = labels == jnp.asarray(g, F32)
        total = jnp.sum(jnp.where(hit, rewards, 0.0), axis=(0, 1, 2), keepdims=True)
        number = jnp.sum(jnp.where(hit, 1.0, 0.0), axis=(0, 1, 2), keepdims=True)
        return jnp.where(hit, total / number, mean)

    mean = jnp.zeros(rewards.shape, F32)
    if groups <= 8:
        for g in range(groups):
            mean = group_mean(g, mean)
    else:
        mean = lax.fori_loop(0, groups, group_mean, mean)
    adv[...] = rewards - mean

    tok = ups_ref.shape[0]
    eye = lax.broadcasted_iota(jnp.int32, (tok, tok), 0) == lax.broadcasted_iota(
        jnp.int32, (tok, tok), 1
    )

    def weigh(q):
        seg = pinfo[q, d, 2:3, :]
        of_seq = adv[q, pl.ds(d, 1), :]
        row = jnp.zeros((1, tok), F32)
        for s in range(seqs):
            row = jnp.where(seg == s, of_seq[:, s : s + 1], row)
        col = jnp.sum(jnp.where(eye, row, 0.0), axis=1, keepdims=True)
        return (uall[q].astype(F32) * col).astype(BF16)

    def dot_nt(a, b):
        return lax.dot_general(a, b, TRAILING, preferred_element_type=F32)

    own = weigh(p)
    wown[...] = own
    back_t = dot_nt(upw_ref[...], own).astype(BF16)
    load_act.wait()

    def grad_block(q):
        part = SCALE * jnp.dot(back_t, act[:, span(q, cols)], preferred_element_type=F32)
        return part.astype(BF16)

    @pl.loop(1, np_)
    def _(s):
        q, dev = plane(s)
        gsend[q] = grad_block(q)
        copy(gsend.at[q], grecv.at[p], g_s.at[q], g_r.at[p], dev).start()

    grecv[p] = grad_block(p)
    load_w.wait()

    def grad_in(q):
        mine = weigh(q)
        back = dot_nt(mine, upw_ref[...]).astype(BF16)
        base = dot_nt(mine, w[...]).astype(BF16)
        adapter = jnp.dot(back, down_ref[:, span(e, cols)], preferred_element_type=F32)
        return (base.astype(F32) + SCALE * adapter).astype(BF16)

    @pl.loop(1, np_)
    def _(s):
        q, dev = plane(s)
        copy(ups_ref, uall.at[q], u_s.at[q], u_r.at[q], dev).wait_recv()
        stage[q] = grad_in(q)
        copy(stage.at[q], out_hbm.at[:, span(p, cols)], out_s.at[q], out_r.at[p], dev).start()

    stage[p] = grad_in(p)
    keep = pltpu.make_async_copy(stage.at[p], out_hbm.at[:, span(p, cols)], load_sem.at[2])
    keep.start()

    arrive(*da)
    width = down_ref.shape[1]
    low_t = lax.fori_loop(
        0,
        nf,
        lambda i, acc: acc + dot_nt(dall[i], act[:, span(i, width)]),
        jnp.zeros((rank, tok), F32),
    ).astype(BF16)
    part = SCALE * jnp.dot(low_t, wown[...], preferred_element_type=F32)
    if np_ > chunks:
        usend[...] = jnp.zeros(usend.shape, F32)
    usend[0:chunks] = part.reshape(chunks, 8, values)
    send(*ur, p)
    urecv[p] = usend[p]

    arrive(*gr)
    zs[d] = lax.fori_loop(
        0, np_, lambda i, acc: acc + grecv[i].astype(F32), jnp.zeros((rank, cols), F32)
    ).astype(BF16)
    send(*zg, d)
    arrive(*ur)
    zu[d] = lax.fori_loop(0, np_, lambda i, acc: acc + urecv[i], jnp.zeros((8, values), F32))
    send(*zp, d)
    arrive(*zg)
    total = jnp.zeros((rank, cols), F32)
    for i in range(nd):
        total = total + zs[i].astype(F32)
    fin[e] = total.astype(BF16)
    send(*fg, e)
    arrive(*zp)
    up_total = jnp.zeros((8, values), F32)
    for i in range(nd):
        up_total = up_total + zu[i]
    square = jnp.sum(total * total, axis=(0, 1), keepdims=True) + jnp.sum(
        up_total * up_total, axis=(0, 1), keepdims=True
    )
    fu[p, :, 0:values] = up_total
    fu[p, :, values:] = jnp.broadcast_to(square, (8, LANES))
    send(*fp, p)

    arrive(*fp)
    squares = jnp.sum(fu[:, 0:1, values : values + 1], axis=0)
    count = F32(rank * act.shape[1] + rank * values)
    factor = jnp.minimum(F32(1.0), jnp.sqrt(count) / (jnp.sqrt(squares) + F32(1e-6)))
    su_ref[...] = fu[0:chunks, :, 0:values].reshape(rank, values) * factor
    arrive(*fg)
    for i in range(ne):
        sd_ref[:, i * cols : (i + 1) * cols] = fin[i].astype(F32) * factor

    keep.wait()
    arrive(*og)
    sent(*zi, d)
    sent(*pi, p)
    sent(*ua, p)
    sent(*da, f)
    sent(*gr, p)
    sent(*ur, p)
    sent(*zg, d)
    sent(*zp, d)
    sent(*fg, e)
    sent(*fp, p)
    sent(*og, p)


def local(
    activations,
    upstream,
    segment,
    reward,
    prompt_group_index,
    frozen_value_weight,
    adapter_down_weight,
    adapter_up_weight,
):
    nf, nd, ne = lax.axis_size("fsdp"), lax.axis_size("dp"), lax.axis_size("engine")
    np_ = nf * ne
    seqs = reward.shape[0]
    groups = seqs * nf * nd * ne // GSIZE
    tok, model = activations.shape
    values = upstream.shape[1]
    cols = frozen_value_weight.shape[0]
    width, rank = adapter_down_weight.shape

    def line(x, fill):
        return jnp.pad(x.astype(F32).reshape(1, -1), ((0, 0), (0, LANES - x.size)), constant_values=fill)

    info = jnp.concatenate(
        [line(reward, 0.0), line(prompt_group_index, -1.0), line(segment, 0.0), jnp.zeros((5, LANES), F32)]
    )
    vmem = pl.BlockSpec(memory_space=pltpu.VMEM)
    anym = pl.BlockSpec(memory_space=pl.ANY)
    dma = pltpu.SemaphoreType.DMA
    plane2 = [dma((np_,)), dma((np_,))]
    line2 = [dma((nd,)), dma((nd,))]
    out, sd, su = pl.pallas_call(
        functools.partial(kernel, (nf, nd, ne, seqs, groups)),
        out_shape=(
            jax.ShapeDtypeStruct((tok, model), BF16),
            jax.ShapeDtypeStruct((rank, width), F32),
            jax.ShapeDtypeStruct((rank, values), F32),
        ),
        in_specs=[anym, vmem, vmem, anym, vmem, vmem],
        out_specs=(anym, vmem, vmem),
        scratch_shapes=[
            pltpu.VMEM((tok, model), BF16),
            pltpu.VMEM((cols, values), BF16),
            pltpu.VMEM((nd, 8, LANES), F32),
            pltpu.VMEM((np_, nd, 8, LANES), F32),
            pltpu.VMEM((np_, nd, LANES), F32),
            pltpu.VMEM((np_, tok, values), BF16),
            pltpu.VMEM((nf, rank, width), BF16),
            pltpu.VMEM((tok, values), BF16),
            pltpu.VMEM((np_, rank, cols), BF16),
            pltpu.VMEM((np_, rank, cols), BF16),
            pltpu.VMEM((np_, 8, values), F32),
            pltpu.VMEM((np_, 8, values), F32),
            pltpu.VMEM((nd, rank, cols), BF16),
            pltpu.VMEM((nd, 8, values), F32),
            pltpu.VMEM((ne, rank, cols), BF16),
            pltpu.VMEM((np_, 8, values + LANES), F32),
            pltpu.VMEM((np_, tok, cols), BF16),
            dma((3,)),
        ]
        + line2
        + plane2
        + plane2
        + [dma((nf,)), dma((nf,))]
        + plane2
        + plane2
        + line2
        + line2
        + [dma((ne,)), dma((ne,))]
        + plane2
        + plane2,
        compiler_params=pltpu.CompilerParams(
            collective_id=0, has_side_effects=True, vmem_limit_bytes=48 * 1024 * 1024
        ),
        cost_estimate=pl.CostEstimate(
            flops=4 * tok * model * values, bytes_accessed=6 * tok * model, transcendentals=0
        ),
    )(activations, upstream, info, frozen_value_weight, adapter_down_weight.T, adapter_up_weight)
    return out, sd.T, su


def solution(mesh):
    everything = ("fsdp", "dp", "engine")
    return jax.shard_map(
        local,
        mesh=mesh,
        in_specs=(
            P(everything, None),
            P(everything, None),
            P(everything, None),
            P(everything),
            P(everything, None),
            P(("fsdp", "engine"), None),
            P("fsdp", None),
            P(),
        ),
        out_specs=(P(everything, None), P("fsdp", None), P()),
        check_vma=False,
    )
```

time: 237 us -> 87.5 us (0.37)
  waiting for transfers between devices: 153 us -> 0 us
  Pallas kernels: 0 us -> 77.8 us
  blocking collectives: 42 us -> 0 us
  matrix products: 16.7 us -> 0 us
  between operations: 16.9 us -> 0.65 us
  local copies, waits for them, and re-layouts: 0.02 us -> 6.76 us
  other arithmetic: 7.64 us -> 2.04 us
    psum x1 -> x0, waiting for transfers between devices: 152 us -> none  [local(): lax.psum((down_gradient, up_gradient), ('fsdp', 'dp', 'engine'))]
    pallas_call x0 -> x1, Pallas kernels: none -> 77.8 us  [local(): pl.pallas_call(functools.partial(kernel, (nf, nd, ne, seqs, groups)), out...]
    psum x1 -> x0, blocking collectives: 42 us -> none  [local(): lax.psum((group_sum, group_count), ('fsdp', 'dp', 'engine'))]
    dot_general x8 -> x0, matrix products: 16.7 us -> none  [the longest x1 6.3 us: local(): lax.dot_general(advantage_weighted, lax.all_gather(frozen_value_weight, (...]
    unnamed x8 -> x11, local copies, waits for them, and re-layouts: 0.02 us -> 6.69 us
    reduce_sum x3 -> x0, other arithmetic: 5.09 us -> none  [the longest x1 2.73 us: local(): jnp.sum(summed_down * summed_down) + jnp.sum(summed_up * summed_up)]
    mul x2 -> x0, other arithmetic: 2.54 us -> none  [local(): return (input_gradient, factor * own_rows, factor * summed_up)]
  transfers between devices with their start and end apart: 3 -> 0, of which waited for: 1 -> 0; matrix products, arithmetic and copies ran while one was open for 6% -> 0% of each run, Pallas kernels for 0% -> 0%
where the time goes in v1:
time: 87.5 us; the launch traced here: 87.2 us
  Pallas kernels  77.8 us (89%)
  local copies, waits for them, and re-layouts  6.76 us (8%)
  other arithmetic  2.04 us (2%)
    pallas_call x1, Pallas kernels, local(): pl.pallas_call(functools.partial(kernel, (nf, nd, ne, seqs, groups)), out...  77.8 us
    unnamed x11, local copies, waits for them, and re-layouts  6.69 us

profile of v1, /device:TPU:0, one launch (start us, length us, event | category | flops | bytes accessed | tf_op | source)
XLA Modules:
  0.0 87.2 jit_solution(16595300480076280471)
XLA Ops:
  0.6 0.7 convert_element_type.7
  1.3 0.7 convert_bitcast_fusion
  1.9 0.1 pad.12.clone
  2.0 0.7 fusion.1.info_ref
  2.8 0.0 copy-start
  2.8 1.2 %copy-done = bf16[1024,512]{1,0:T(8,128)(2,1)S(1)} copy-done((bf16[1024,512]{1,0:T(8,128)(2,1)S(1)}, bf16[1024,512]{1,0:T(8,128)(2,1)}, u32[]{:S(2)}) %copy-start) | copy-done | bytes 1048600
  4.0 0.0 copy-start.1
  4.0 0.9 %copy-done.1 = bf16[2048,64]{0,1:T(8,128)(2,1)S(1)} copy-done((bf16[2048,64]{0,1:T(8,128)(2,1)S(1)}, bf16[2048,64]{0,1:T(8,128)(2,1)}, u32[]{:S(2)}) %copy-start.1) | copy-done | bytes 262168
  4.9 0.0 copy-start.2
  4.9 0.9 %copy-done.2 = bf16[128,512]{1,0:T(8,128)(2,1)S(1)} copy-done((bf16[128,512]{1,0:T(8,128)(2,1)S(1)}, bf16[128,512]{1,0:T(8,128)(2,1)}, u32[]{:S(2)}) %copy-start.2) | copy-done | bytes 131096
  5.8 0.0 copy-start.3
  5.8 0.8 copy-done.3
  6.7 77.8 %shard_map.103 = (bf16[128,8192]{1,0:T(8,128)(2,1)S(1)}, f32[64,2048]{1,0:T(8,128)S(1)}, f32[64,512]{1,0:T(8,128)S(1)}) custom-call(bf16[128,8192]{1,0:T(8,128)(2,1)} %act_hbm.1, bf16[128,512]{1,0:T(8,128)(2,1)S(1)} %copy-done.2, f32[8,128]{1,0:T(8,128)S(1)} %fusion.1.info_ref, bf16[1024,512]{1,0:T(8,128)(2,1)S(1)} %copy-done, bf16[64,2048]{1,0:T(8,128)(2,1)S(1)} %bitcast.6, ...), custom_call_target="tpu_custom_call" | custom-call | flops 2147483648 | bytes 6291456 | tf_op jit(solution)/shard_map/pallas_call | solution.py:331
  84.5 1.3 %copy.14 = bf16[128,8192]{1,0:T(8,128)(2,1)} copy(bf16[128,8192]{1,0:T(8,128)(2,1)S(1)} %get-tuple-element.12) | data formatting | bytes 4194304
  85.8 0.8 copy.15
  86.6 0.7 copy.16
  (1 shorter events, 0.0 us)
Async XLA Ops:
  2.8 1.2 %copy-start = (bf16[1024,512]{1,0:T(8,128)(2,1)S(1)}, bf16[1024,512]{1,0:T(8,128)(2,1)}, u32[]{:S(2)}) copy-start(bf16[1024,512]{1,0:T(8,128)(2,1)} %w_hbm.1) | copy-start | bytes 3145732
  4.0 0.9 %copy-start.1 = (bf16[2048,64]{0,1:T(8,128)(2,1)S(1)}, bf16[2048,64]{0,1:T(8,128)(2,1)}, u32[]{:S(2)}) copy-start(bf16[2048,64]{0,1:T(8,128)(2,1)} %param.14) | copy-start | bytes 786436
  4.9 0.9 %copy-start.2 = (bf16[128,512]{1,0:T(8,128)(2,1)S(1)}, bf16[128,512]{1,0:T(8,128)(2,1)}, u32[]{:S(2)}) copy-start(bf16[128,512]{1,0:T(8,128)(2,1)} %ups_ref.1) | copy-start | bytes 393220
  5.8 0.8 copy-start.3

commit v2 on v1

--- a/solution.py
+++ b/solution.py
@@ -19,16 +19,19 @@
 def kernel(
     dims,
     act_hbm,
-    ups_ref,
-    info_ref,
+    ups_hbm,
+    reward_ref,
+    group_ref,
+    seg_ref,
     w_hbm,
-    down_ref,
-    upw_ref,
+    down_hbm,
+    upw_hbm,
     out_hbm,
     sd_ref,
     su_ref,
     act,
     w,
+    upw_ref,
     zinfo,
     pinfo,
     adv,
@@ -36,8 +39,10 @@
     dall,
     wown,
     gsend,
+    gmate,
     grecv,
     usend,
+    umate,
     urecv,
     zs,
     zu,
@@ -53,8 +58,12 @@
     u_r,
     d_s,
     d_r,
+    gm_s,
+    gm_r,
     g_s,
     g_r,
+    um_s,
+    um_r,
     up_s,
     up_r,
     zs_s,
@@ -72,6 +81,11 @@
     np_ = nf * ne
     f, d, e = lax.axis_index("fsdp"), lax.axis_index("dp"), lax.axis_index("engine")
     p = f * ne + e
+    half = np_ // 2
+    fb = lax.rem(f, 2)
+    h = (f // 2) * ne + e
+    other = 1 - 2 * fb
+    sib = {"fsdp": f + other}
     cols = w.shape[0]
     rank, values = upw_ref.shape
     chunks = rank // 8
@@ -94,8 +108,16 @@
         q = lax.rem(d + s, nd)
         return q, {"dp": q}
 
+    def same(s):
+        k = lax.rem(h + s, half)
+        g = 2 * (k // ne) + fb
+        return g * ne + lax.rem(k, ne), {"fsdp": g, "engine": lax.rem(k, ne)}
+
+    def mate(q):
+        return q + other * ne
+
     def fs(s):
-        q = lax.rem(f + s, nf)
+        q = 2 * lax.rem(f // 2 + s, nf // 2) + fb
         return q, {"fsdp": q}
 
     def eng(s):
@@ -110,10 +132,22 @@
     def span(q, width):
         return pl.ds(pl.multiple_of(q * width, LANES), width)
 
-    load_act = pltpu.make_async_copy(act_hbm, act, load_sem.at[0])
-    load_w = pltpu.make_async_copy(w_hbm, w, load_sem.at[1])
-    load_act.start()
-    load_w.start()
+    def load(src, dst, i):
+        got = pltpu.make_async_copy(src, dst, load_sem.at[i])
+        got.start()
+        return got
+
+    load_ups = load(ups_hbm, uall.at[p], 3)
+    load_upw = load(upw_hbm, upw_ref, 4)
+    load_act = load(act_hbm, act, 0)
+    load_down = load(down_hbm, dall.at[f], 5)
+    load_w = load(w_hbm, w, 1)
+
+    zinfo[d] = jnp.zeros(zinfo.shape[1:], F32)
+    zinfo[d, 0:1, 0:seqs] = reward_ref[...]
+    zinfo[d, 1:2, :] = jnp.full((1, LANES), -1.0, F32)
+    zinfo[d, 1:2, 0:seqs] = group_ref[...].astype(F32)
+    zinfo[d, 2:3, :] = seg_ref[...].astype(F32)
 
     barrier = pltpu.get_barrier_semaphore()
     each(nd, lambda s: pl.semaphore_signal(barrier, inc=1, device_id=line(s)[1], device_id_type=MESH))
@@ -141,27 +175,40 @@
 
         each(count, go)
 
-    zi = (line, nd, lambda q: info_ref, lambda q: zinfo.at[q], zinfo_s, zinfo_r)
+    zi = (line, nd, lambda q: zinfo.at[d], lambda q: zinfo.at[q], zinfo_s, zinfo_r)
     pi = (plane, np_, lambda q: zinfo, lambda q: pinfo.at[q], pinfo_s, pinfo_r)
-    ua = (plane, np_, lambda q: ups_ref, lambda q: uall.at[q], u_s, u_r)
-    da = (fs, nf, lambda q: down_ref, lambda q: dall.at[q], d_s, d_r)
-    gr = (plane, np_, lambda q: gsend.at[q], lambda q: grecv.at[q], g_s, g_r)
-    ur = (plane, np_, lambda q: usend.at[q], lambda q: urecv.at[q], up_s, up_r)
+    ua = (same, half, lambda q: uall.at[p], lambda q: uall.at[q], u_s, u_r)
+    da = (fs, nf // 2, lambda q: dall.at[f], lambda q: dall.at[q], d_s, d_r)
+    gr = (same, half, lambda q: gsend.at[q], lambda q: grecv.at[q], g_s, g_r)
+    ur = (same, half, lambda q: usend.at[q], lambda q: urecv.at[q], up_s, up_r)
     zg = (line, nd, lambda q: zs.at[d], lambda q: zs.at[q], zs_s, zs_r)
     zp = (line, nd, lambda q: zu.at[d], lambda q: zu.at[q], zu_s, zu_r)
     fg = (eng, ne, lambda q: fin.at[e], lambda q: fin.at[q], fin_s, fin_r)
     fp = (plane, np_, lambda q: fu.at[p], lambda q: fu.at[q], fu_s, fu_r)
     og = (plane, np_, lambda q: stage.at[q], lambda q: out_hbm.at[:, span(q, cols)], out_s, out_r)
 
+    def hand_up(q):
+        return copy(uall.at[q], uall.at[q], u_s.at[mate(q)], u_r.at[q], sib)
+
+    def hand_down(g):
+        return copy(dall.at[g], dall.at[g], d_s.at[g + other], d_r.at[g], sib)
+
+    def hand_grad(q):
+        return copy(gsend.at[q], gmate.at[q], gm_s.at[q], gm_r.at[q], sib)
+
+    def hand_part(q):
+        return copy(usend.at[q], umate.at[q], um_s.at[q], um_r.at[q], sib)
+
     send(*zi, d)
-    zinfo[d] = info_ref[...]
     arrive(*zi)
     send(*pi, p)
+    load_ups.wait()
     send(*ua, p)
+    hand_up(p).start()
+    load_down.wait()
     send(*da, f)
+    hand_down(f).start()
     pinfo[p] = zinfo[...]
-    uall[p] = ups_ref[...]
-    dall[f] = down_ref[...]
     arrive(*pi)
 
     rewards = pinfo[:, :, 0, :]
@@ -181,7 +228,7 @@
         mean = lax.fori_loop(0, groups, group_mean, mean)
     adv[...] = rewards - mean
 
-    tok = ups_ref.shape[0]
+    tok = act.shape[0]
     eye = lax.broadcasted_iota(jnp.int32, (tok, tok), 0) == lax.broadcasted_iota(
         jnp.int32, (tok, tok), 1
     )
@@ -200,42 +247,71 @@
 
     own = weigh(p)
     wown[...] = own
+    load_upw.wait()
     back_t = dot_nt(upw_ref[...], own).astype(BF16)
     load_act.wait()
 
     def grad_block(q):
-        part = SCALE * jnp.dot(back_t, act[:, span(q, cols)], preferred_element_type=F32)
-        return part.astype(BF16)
-
-    @pl.loop(1, np_)
-    def _(s):
-        q, dev = plane(s)
-        gsend[q] = grad_block(q)
+        return SCALE * jnp.dot(back_t, act[:, span(q, cols)], preferred_element_type=F32)
+
+    @pl.loop(1, half + 1)
+    def _(s):
+        q = mate(same(s)[0])
+        gsend[q] = grad_block(q).astype(BF16)
+        hand_grad(q).start()
+
+    def chip_block(q):
+        part = grad_block(q)
+        hand_grad(q).wait_recv()
+        return (part + gmate[q].astype(F32)).astype(BF16)
+
+    @pl.loop(1, half)
+    def _(s):
+        q, dev = same(s)
+        gsend[q] = chip_block(q)
         copy(gsend.at[q], grecv.at[p], g_s.at[q], g_r.at[p], dev).start()
 
-    grecv[p] = grad_block(p)
+    grecv[p] = chip_block(p)
     load_w.wait()
 
     def grad_in(q):
         mine = weigh(q)
         back = dot_nt(mine, upw_ref[...]).astype(BF16)
         base = dot_nt(mine, w[...]).astype(BF16)
-        adapter = jnp.dot(back, down_ref[:, span(e, cols)], preferred_element_type=F32)
+        adapter = jnp.dot(back, dall[f, :, span(e, cols)], preferred_element_type=F32)
         return (base.astype(F32) + SCALE * adapter).astype(BF16)
 
-    @pl.loop(1, np_)
-    def _(s):
-        q, dev = plane(s)
-        copy(ups_ref, uall.at[q], u_s.at[q], u_r.at[q], dev).wait_recv()
+    def send_in(q, dev):
         stage[q] = grad_in(q)
         copy(stage.at[q], out_hbm.at[:, span(p, cols)], out_s.at[q], out_r.at[p], dev).start()
+
+    @pl.loop(1, half)
+    def _(s):
+        q, dev = same(s)
+        copy(uall.at[p], uall.at[q], u_s.at[q], u_r.at[q], dev).wait_recv()
+        hand_up(q).start()
+        send_in(q, dev)
+
+    def pass_down(s):
+        g, dev = fs(s)
+        copy(dall.at[f], dall.at[g], d_s.at[g], d_r.at[g], dev).wait_recv()
+        hand_down(g).start()
+
+    each(nf // 2, pass_down)
+
+    @pl.loop(1, half + 1)
+    def _(s):
+        q, dev = same(s)
+        hand_up(mate(q)).wait_recv()
+        send_in(mate(q), {"fsdp": dev["fsdp"] + other, "engine": dev["engine"]})
 
     stage[p] = grad_in(p)
     keep = pltpu.make_async_copy(stage.at[p], out_hbm.at[:, span(p, cols)], load_sem.at[2])
     keep.start()
 
-    arrive(*da)
-    width = down_ref.shape[1]
+    hand_down(f + other).wait_recv()
+    each(nf // 2, lambda s: hand_down(fs(s)[0] + other).wait_recv())
+    width = dall.shape[2]
     low_t = lax.fori_loop(
         0,
         nf,
@@ -246,16 +322,30 @@
     if np_ > chunks:
         usend[...] = jnp.zeros(usend.shape, F32)
     usend[0:chunks] = part.reshape(chunks, 8, values)
-    send(*ur, p)
-    urecv[p] = usend[p]
+    @pl.loop(1, half + 1)
+    def _(s):
+        hand_part(mate(same(s)[0])).start()
+
+    @pl.loop(1, half)
+    def _(s):
+        q, dev = same(s)
+        hand_part(q).wait_recv()
+        usend[q] = usend[q] + umate[q]
+        copy(usend.at[q], urecv.at[p], up_s.at[q], up_r.at[p], dev).start()
+
+    hand_part(p).wait_recv()
+    urecv[p] = usend[p] + umate[p]
+
+    def peer(k):
+        return (2 * (k // ne) + fb) * ne + lax.rem(k, ne)
 
     arrive(*gr)
     zs[d] = lax.fori_loop(
-        0, np_, lambda i, acc: acc + grecv[i].astype(F32), jnp.zeros((rank, cols), F32)
+        0, half, lambda i, acc: acc + grecv[peer(i)].astype(F32), jnp.zeros((rank, cols), F32)
     ).astype(BF16)
     send(*zg, d)
     arrive(*ur)
-    zu[d] = lax.fori_loop(0, np_, lambda i, acc: acc + urecv[i], jnp.zeros((8, values), F32))
+    zu[d] = lax.fori_loop(0, half, lambda i, acc: acc + urecv[peer(i)], jnp.zeros((8, values), F32))
     send(*zp, d)
     arrive(*zg)
     total = jnp.zeros((rank, cols), F32)
@@ -291,6 +381,18 @@
     sent(*da, f)
     sent(*gr, p)
     sent(*ur, p)
+
+    @pl.loop(0, half)
+    def _(s):
+        q = same(s)[0]
+        hand_up(q).wait_send()
+        hand_grad(mate(q)).wait_send()
+        hand_part(mate(q)).wait_send()
+
+    @pl.loop(0, nf // 2)
+    def _(s):
+        hand_down(fs(s)[0]).wait_send()
+
     sent(*zg, d)
     sent(*zp, d)
     sent(*fg, e)
@@ -317,12 +419,6 @@
     cols = frozen_value_weight.shape[0]
     width, rank = adapter_down_weight.shape
 
-    def line(x, fill):
-        return jnp.pad(x.astype(F32).reshape(1, -1), ((0, 0), (0, LANES - x.size)), constant_values=fill)
-
-    info = jnp.concatenate(
-        [line(reward, 0.0), line(prompt_group_index, -1.0), line(segment, 0.0), jnp.zeros((5, LANES), F32)]
-    )
     vmem = pl.BlockSpec(memory_space=pltpu.VMEM)
     anym = pl.BlockSpec(memory_space=pl.ANY)
     dma = pltpu.SemaphoreType.DMA
@@ -335,11 +431,12 @@
             jax.ShapeDtypeStruct((rank, width), F32),
             jax.ShapeDtypeStruct((rank, values), F32),
         ),
-        in_specs=[anym, vmem, vmem, anym, vmem, vmem],
+        in_specs=[anym, anym, vmem, vmem, vmem, anym, anym, anym],
         out_specs=(anym, vmem, vmem),
         scratch_shapes=[
             pltpu.VMEM((tok, model), BF16),
             pltpu.VMEM((cols, values), BF16),
+            pltpu.VMEM((rank, values), BF16),
             pltpu.VMEM((nd, 8, LANES), F32),
             pltpu.VMEM((np_, nd, 8, LANES), F32),
             pltpu.VMEM((np_, nd, LANES), F32),
@@ -348,6 +445,8 @@
             pltpu.VMEM((tok, values), BF16),
             pltpu.VMEM((np_, rank, cols), BF16),
             pltpu.VMEM((np_, rank, cols), BF16),
+            pltpu.VMEM((np_, rank, cols), BF16),
+            pltpu.VMEM((np_, 8, values), F32),
             pltpu.VMEM((np_, 8, values), F32),
             pltpu.VMEM((np_, 8, values), F32),
             pltpu.VMEM((nd, rank, cols), BF16),
@@ -355,12 +454,14 @@
             pltpu.VMEM((ne, rank, cols), BF16),
             pltpu.VMEM((np_, 8, values + LANES), F32),
             pltpu.VMEM((np_, tok, cols), BF16),
-            dma((3,)),
+            dma((6,)),
         ]
         + line2
         + plane2
         + plane2
         + [dma((nf,)), dma((nf,))]
+        + plane2
+        + plane2
         + plane2
         + plane2
         + line2
@@ -369,12 +470,21 @@
         + plane2
         + plane2,
         compiler_params=pltpu.CompilerParams(
-            collective_id=0, has_side_effects=True, vmem_limit_bytes=48 * 1024 * 1024
+            collective_id=0, has_side_effects=True, vmem_limit_bytes=60 * 1024 * 1024
         ),
         cost_estimate=pl.CostEstimate(
             flops=4 * tok * model * values, bytes_accessed=6 * tok * model, transcendentals=0
         ),
-    )(activations, upstream, info, frozen_value_weight, adapter_down_weight.T, adapter_up_weight)
+    )(
+        activations,
+        upstream,
+        reward.reshape(1, seqs),
+        prompt_group_index.reshape(1, seqs),
+        segment,
+        frozen_value_weight,
+        adapter_down_weight.T,
+        adapter_up_weight,
+    )
     return out, sd.T, su
 
 

time: 87.5 us -> 67.7 us (0.77)
  Pallas kernels: 77.8 us -> 62.3 us
  local copies, waits for them, and re-layouts: 6.76 us -> 4.62 us
  other arithmetic: 2.04 us -> 0 us
    pallas_call x1, Pallas kernels: 77.8 us -> 62.3 us  [local(): pl.pallas_call(functools.partial(kernel, (nf, nd, ne, seqs, groups)), out...]
    unnamed x11 -> x7, local copies, waits for them, and re-layouts: 6.69 us -> 4.62 us
where the time goes in v2:
time: 67.7 us; the launch traced here: 67.6 us
  Pallas kernels  62.3 us (92%)
  local copies, waits for them, and re-layouts  4.62 us (7%)
    pallas_call x1, Pallas kernels, local(): pl.pallas_call(functools.partial(kernel, (nf, nd, ne, seqs, groups)), out...  62.3 us
    unnamed x7, local copies, waits for them, and re-layouts  4.62 us

profile of v2, /device:TPU:0, one launch (start us, length us, event | category | flops | bytes accessed | tf_op | source)
XLA Modules:
  0.0 67.6 jit_solution(14190293732867288348)
XLA Ops:
  0.6 62.3 %shard_map.103 = (bf16[128,8192]{1,0:T(8,128)(2,1)}, f32[64,2048]{1,0:T(8,128)}, f32[64,512]{1,0:T(8,128)}) custom-call(bf16[128,8192]{1,0:T(8,128)(2,1)} %act_hbm.1, bf16[128,512]{1,0:T(8,128)(2,1)} %ups_hbm.1, f32[1,4]{1,0:T(1,128)} %bitcast.6, s32[1,4]{1,0:T(1,128)} %bitcast.7, s32[1,128]{1,0:T(1,128)} %seg_ref.1, bf16[1024,512]{1,0:T(8,128)(2,1)} %w_hbm.1, ...), custom_call_target="tpu_custom_call" | custom-call | flops 2147483648 | bytes 6291456 | tf_op jit(solution)/shard_map/pallas_call | solution.py:427
  62.9 0.0 copy-start
  62.9 0.0 copy-start.1
  62.9 3.2 %copy.14 = bf16[128,8192]{1,0:T(8,128)(2,1)} copy(bf16[128,8192]{1,0:T(8,128)(2,1)} %get-tuple-element.12) | data formatting | bytes 4194304
  66.1 0.0 copy-done
  66.1 0.8 %copy.15 = f32[2048,64]{0,1:T(8,128)} copy(f32[2048,64]{0,1:T(8,128)S(1)} %bitcast.4) | data formatting | bytes 1048576
  66.9 0.0 copy-done.1
  66.9 0.7 copy.16
Async XLA Ops:
  62.9 3.2 %copy-start = (f32[64,2048]{1,0:T(8,128)S(1)}, f32[64,2048]{1,0:T(8,128)}, u32[]{:S(2)}) copy-start(f32[64,2048]{1,0:T(8,128)} %get-tuple-element.7) | copy-start | bytes 1572868
  62.9 4.0 %copy-start.1 = (f32[64,512]{1,0:T(8,128)S(1)}, f32[64,512]{1,0:T(8,128)}, u32[]{:S(2)}) copy-start(f32[64,512]{1,0:T(8,128)} %get-tuple-element.14) | copy-start | bytes 393220
